TPU v7x, 512 devices: a whole 4x8x8 slice. The times are simulated.
512 devices in a mesh: dp: 64 (over z_lo, x, y), tensor: 8 (over z_hi, core).
Axes of the slice: x: 4, y: 8, z: 8 (z_hi: 4, z_lo: 2; z = z_hi * 2 + z_lo), core: 2. Of those that a mesh axis runs over, the one named last changes fastest.
Arguments:
- grad_part: bfloat16 [64, 4, 192, 5120], P('dp', None, None, 'tensor'), may hold values from -16 to 16
- hess_part: bfloat16 [64, 4, 192, 5120], P('dp', None, None, 'tensor'), may hold values from 0.5 to 5
- momentum: float32 [4, 192, 5120], P(None, 'dp', 'tensor'), may hold values from -18 to 18
- hessian: float32 [4, 192, 5120], P(None, 'dp', 'tensor'), may hold values from 0.2 to 2
- master: float32 [4, 192, 5120], P(None, 'dp', 'tensor'), may hold values from -0.078125 to 0.078125
- step: int32 [1], replicated, may hold values from 1 to 100
- refresh: int32 [4], replicated, may hold values from 0 to 1, as said below
Outputs:
- new_momentum: float32 [4, 192, 5120], P(None, 'dp', 'tensor')
- new_hessian: float32 [4, 192, 5120], P(None, 'dp', 'tensor')
- new_master: float32 [4, 192, 5120], P(None, 'dp', 'tensor')
- weights: bfloat16 [4, 192, 5120], P(None, None, 'tensor')
- clip_fraction: float32 [1], replicated
Inputs may be any that keep to these rules, and one draw needn't show every extreme that they name: `refresh`: each flag is 0 or 1; at least one layer has 1 and at least one has 0.
All inputs are finite; a program needn't handle non-finite values.
Results may differ from a plain program's by a relative error of at most 0.001.
Values may be sent and summed in bfloat16 or wider, within the bound.
No kernel may reach another device: no remote copies, remote signals or barrier semaphores. Data moves between devices by JAX's collectives and lax.ppermute only.
A program may use at most 64 MiB of HBM per device.

v0:
```python
import jax
import jax.numpy as jnp
from jax import lax
from jax.sharding import PartitionSpec as P

BETA_ONE = 0.965
BETA_TWO = 0.99
RHO_SCALE = 0.5
LEARN_RATE = 0.0006
DECAY_RATE = 0.1


def local(grad_part, hess_part, momentum, hessian, master, step, refresh):
    grad_local = grad_part[0].astype(jnp.float32)
    hess_local = hess_part[0].astype(jnp.float32)
    grad_sum, hess_sum = (
        lax.psum_scatter(grad_local, "dp", scatter_dimension=1, tiled=True),
        lax.psum_scatter(hess_local, "dp", scatter_dimension=1, tiled=True),
    )
    new_momentum = BETA_ONE * momentum + (1.0 - BETA_ONE) * grad_sum
    layer_flags = (refresh > 0)[:, None, None]
    new_hessian = jnp.where(layer_flags, BETA_TWO * hessian + (1.0 - BETA_TWO) * hess_sum, hessian)
    correction = 1.0 - jnp.power(jnp.float32(BETA_ONE), step[0].astype(jnp.float32))
    ratios = new_momentum / correction / (RHO_SCALE * new_hessian)
    clipped = jnp.clip(ratios, -1.0, 1.0)
    new_master = master * (1.0 - LEARN_RATE * DECAY_RATE) - LEARN_RATE * clipped
    weights = lax.all_gather(new_master.astype(jnp.bfloat16), "dp", axis=1, tiled=True)
    clipped_count = jnp.sum((jnp.abs(ratios) >= 1.0).astype(jnp.float32))
    all_clipped = lax.psum(clipped_count, ("dp", "tensor"))
    entries = ratios.size * lax.axis_size("dp") * lax.axis_size("tensor")
    clip_fraction = jnp.reshape(all_clipped / entries, (1,))
    return (new_momentum, new_hessian, new_master, weights, clip_fraction)


def solution(mesh):
    in_specs = (
        P("dp", None, None, "tensor"),
        P("dp", None, None, "tensor"),
        P(None, "dp", "tensor"),
        P(None, "dp", "tensor"),
        P(None, "dp", "tensor"),
        P(),
        P(),
    )
    out_specs = (
        P(None, "dp", "tensor"),
        P(None, "dp", "tensor"),
        P(None, "dp", "tensor"),
        P(None, None, "tensor"),
        P(),
    )
    return jax.shard_map(local, mesh=mesh, in_specs=in_specs, out_specs=out_specs, check_vma=False)
```

profile of v0, /device:TPU:1, one launch (start us, length us, event | category | flops | bytes accessed | tf_op | source)
XLA Modules:
  0.0 901.3 jit_solution(6631353973265179613)
XLA Ops:
  7.2 0.0 all-reduce.5.cloned.1.call-start
  7.2 4.9 bitcast_convert_fusion
  12.1 0.0 copy-start.3
  12.1 0.0 copy-start
  12.1 0.0 copy-start.1
  12.1 0.0 copy-start.2
  12.1 0.0 all-reduce.5.cloned.1.call-update
  12.8 1.3 dynamic-slice
  14.8 0.0 copy-done.3
  14.8 577.6 %all-reduce.5.cloned.1.call-done = (f32[4,192,640]{2,0,1:T(4,128)}, f32[4,192,640]{2,0,1:T(4,128)}) async-done(((f32[4,192,640]{2,0,1:T(4,128)}, f32[4,192,640]{2,0,1:T(4,128)}), (f32[4,192,640]{2,0,1:T(4,128)}, f32[4,192,640]{2,0,1:T(4,128)})) %all-reduce.5.cloned.1.call-update) | async-done | bytes 3932176
  592.5 0.0 copy-done
  592.5 0.0 copy-done.1
  592.5 2.1 convert_reduce_fusion
  594.5 0.0 copy-done.2
  594.5 0.6 fusion.5
  595.1 129.4 %all_gather.3 = bf16[4,192,640]{2,0,1:T(4,128)(2,1)S(1)} all-gather(bf16[4,3,640]{2,0,1:T(4,128)(2,1)S(1)} %get-tuple-element.16), channel_id=1, replica_groups=mesh['dp'=64,'tensor'=8] {'dp'}, dimensions={1}, use_global_device_ids=true | all-gather | bytes 998400 | tf_op jit(solution)/shard_map/all_gather | solution.py:27
  724.6 1.1 copy.17
  725.6 167.0 %psum.7 = f32[]{:T(128)} all-reduce(f32[]{:T(128)} %get-tuple-element.12), channel_id=1, replica_groups=mesh['dp'=64,'tensor'=8] {'dp','tensor'}, use_global_device_ids=true, to_apply=%region_3.4 | all-reduce | flops 1 | bytes 8 | tf_op jit(solution)/shard_map/psum | solution.py:29
  (1 shorter events, 0.0 us)
Async XLA Ops:
  7.2 585.3 %all-reduce.5.cloned.1.call-start = ((), (), s32[]{:S(2)}) async-start(), calls=%async_computation | async-start | bytes 7864320
  12.1 2.7 copy-start.3
  12.1 580.3 %copy-start = (f32[4,3,640]{2,0,1:T(4,128)S(1)}, f32[4,3,640]{2,0,1:T(4,128)}, u32[]{:S(2)}) copy-start(f32[4,3,640]{2,0,1:T(4,128)} %param.10) | copy-start | bytes 92164
  12.1 580.3 %copy-start.1 = (f32[4,3,640]{2,0,1:T(4,128)S(1)}, f32[4,3,640]{2,0,1:T(4,128)}, u32[]{:S(2)}) copy-start(f32[4,3,640]{2,0,1:T(4,128)} %param.9) | copy-start | bytes 92164
  12.1 582.4 %copy-start.2 = (f32[4,3,640]{2,0,1:T(4,128)S(1)}, f32[4,3,640]{2,0,1:T(4,128)}, u32[]{:S(2)}) copy-start(f32[4,3,640]{2,0,1:T(4,128)} %param.11) | copy-start | bytes 92164
Sparse Core Ops, SparseCore 0:
  12.3 580.1 all-reduce.4
where the time goes:
time: 902 us; the launch traced here: 901 us
  waiting for transfers between devices  578 us (64%)
  blocking collectives  296 us (33%)
  between operations  17.2 us (2%)
    unnamed x2, waiting for transfers between devices  578 us
    psum x1, blocking collectives, local(): all_clipped = lax.psum(clipped_count, ('dp', 'tensor'))  167 us
    all_gather x1, blocking collectives, local(): lax.all_gather(new_master.astype(jnp.bfloat16), 'dp', axis=1, tiled=True)  129 us
  transfers between devices with their start and end apart: 1, of which 1 were waited for; matrix products, arithmetic and copies ran while one was open for 0% of the time, Pallas kernels for 0%

commit v1 on v0

v1 whole, which is shorter than its diff:
```python
import jax
import jax.numpy as jnp
from jax import lax
from jax.sharding import Mesh
from jax.sharding import PartitionSpec as P

BETA_ONE = 0.965
BETA_TWO = 0.99
RHO_SCALE = 0.5
LEARN_RATE = 0.0006
DECAY_RATE = 0.1

ZL, X, Y, ZH, CORE = 2, 4, 8, 4, 2
DP = ("zl", "x", "y")
TENSOR = ("zh", "core")
FIRST = ("zl", "x")
BASE = 256.0


def exchange(blocks, axes):
    return lax.all_to_all(blocks, axes, split_axis=0, concat_axis=0, tiled=False)


def digits(count):
    high = jnp.floor(count * (1.0 / BASE))
    return high, count - BASE * high


def local(grad_part, hess_part, momentum, hessian, master, step, refresh):
    layers, rows, cols = grad_part.shape[1:]
    outer, inner = ZL * X, Y
    block, own = rows // outer, rows // (outer * inner)

    flags = (refresh > 0).astype(jnp.int32)
    place = jnp.cumsum(flags) - flags
    slots = layers - 1
    picks = [
        jnp.sum(jnp.where((flags > 0) & (place == s), jnp.arange(layers), 0)) for s in range(slots)
    ]
    hess_used = [lax.dynamic_index_in_dim(hess_part[0], p, 0, keepdims=True) for p in picks]
    stacked = jnp.concatenate([grad_part[0]] + hess_used, axis=0)
    lots = layers + slots
    blocks = stacked.reshape(lots, outer, block, cols).transpose(1, 0, 2, 3)

    came = exchange(blocks, FIRST)
    partial = jnp.sum(came.astype(jnp.float32), axis=0)
    partial = partial.reshape(lots, inner, own, cols).transpose(1, 0, 2, 3)
    came = exchange(partial.reshape(inner, lots * own, cols), "y")
    sums = jnp.sum(came, axis=0).reshape(lots, own, cols)
    grad_sum = sums[:layers]
    hess_sum = jnp.stack(
        [
            lax.dynamic_index_in_dim(sums, layers + jnp.minimum(place[l], slots - 1), 0, keepdims=False)
            for l in range(layers)
        ]
    )

    new_momentum = BETA_ONE * momentum + (1.0 - BETA_ONE) * grad_sum
    layer_flags = (refresh > 0)[:, None, None]
    new_hessian = jnp.where(layer_flags, BETA_TWO * hessian + (1.0 - BETA_TWO) * hess_sum, hessian)
    correction = 1.0 - jnp.power(jnp.float32(BETA_ONE), step[0].astype(jnp.float32))
    ratios = new_momentum / correction / (RHO_SCALE * new_hessian)
    clipped = jnp.clip(ratios, -1.0, 1.0)
    new_master = master * (1.0 - LEARN_RATE * DECAY_RATE) - LEARN_RATE * clipped
    mine = new_master.astype(jnp.bfloat16)
    count = jnp.sum((jnp.abs(ratios) >= 1.0).astype(jnp.float32))

    high, low = digits(count)
    tail = jnp.stack([high, low, high, low]).astype(jnp.bfloat16)
    tail = jnp.broadcast_to(tail[:, None], (4, cols))
    load = jnp.concatenate([mine.reshape(layers * own, cols), tail], axis=0)
    came = exchange(jnp.broadcast_to(load[None], (inner,) + load.shape), "y")
    held = came[:, : layers * own].reshape(inner, layers, own, cols).transpose(1, 0, 2, 3)
    held = held.reshape(layers * block, cols)
    marks = came[:, layers * own : layers * own + 2, 0].astype(jnp.float32)
    count = jnp.sum(marks[:, 0] * BASE + marks[:, 1])

    high, low = digits(count)
    tail = jnp.stack([high, low] * 8).astype(jnp.bfloat16)
    tail = jnp.broadcast_to(tail[:, None], (16, cols))
    load = jnp.concatenate([held, tail], axis=0)
    came = exchange(jnp.broadcast_to(load[None], (outer,) + load.shape), FIRST)
    weights = came[:, : layers * block].reshape(outer, layers, block, cols).transpose(1, 0, 2, 3)
    weights = weights.reshape(layers, rows, cols)
    marks = came[:, layers * block : layers * block + 2, 0].astype(jnp.float32)
    count = jnp.sum(marks[:, 0] * BASE + marks[:, 1])

    came = exchange(jnp.broadcast_to(count, (ZH * CORE, 1, 128)), TENSOR)
    total = jnp.sum(came[:, 0, 0])
    entries = ratios.size * outer * inner * ZH * CORE
    clip_fraction = jnp.reshape(total / entries, (1,))
    return (new_momentum, new_hessian, new_master, weights, clip_fraction)


def solution(mesh):
    fine = Mesh(mesh.devices.reshape(ZL, X, Y, ZH, CORE), DP + TENSOR)
    shards = P(DP, None, None, TENSOR)
    state = P(None, DP, TENSOR)
    in_specs = (shards, shards, state, state, state, P(), P())
    out_specs = (state, state, state, P(None, None, TENSOR), P())
    return jax.shard_map(local, mesh=fine, in_specs=in_specs, out_specs=out_specs, check_vma=False)
```

time: 902 us -> 119 us (0.13)
  waiting for transfers between devices: 578 us -> 14.2 us
  blocking collectives: 296 us -> 52.3 us
  starting transfers between devices: 0.04 us -> 24.2 us
    unnamed x2 -> x0, waiting for transfers between devices: 578 us -> none
    psum x1 -> x0, blocking collectives: 167 us -> none  [local(): all_clipped = lax.psum(clipped_count, ('dp', 'tensor'))]
    all_gather x1 -> x0, blocking collectives: 129 us -> none  [local(): lax.all_gather(new_master.astype(jnp.bfloat16), 'dp', axis=1, tiled=True)]
    all_to_all x0 -> x3, blocking collectives: none -> 52.3 us  [exchange(): lax.all_to_all(blocks, axes, split_axis=0, concat_axis=0, tiled=False)]
    all_to_all x0 -> x2, starting transfers between devices: none -> 24.2 us  [exchange(): lax.all_to_all(blocks, axes, split_axis=0, concat_axis=0, tiled=False)]
    all_to_all x0 -> x2, waiting for transfers between devices: none -> 14.2 us  [exchange(): lax.all_to_all(blocks, axes, split_axis=0, concat_axis=0, tiled=False)]
  transfers between devices with their start and end apart: 1 -> 2, of which waited for: 1 -> 2; matrix products, arithmetic and copies ran while one was open for 0% -> 3% of each run, Pallas kernels for 0% -> 0%
where the time goes in v1:
time: 119 us
  blocking collectives  52.3 us (44%)
  starting transfers between devices  24.2 us (20%)
  between operations  14.4 us (12%)
  waiting for transfers between devices  14.2 us (12%)
  local copies, waits for them, and re-layouts  8.08 us (7%)
  other arithmetic  5.64 us (5%)
    all_to_all x3, blocking collectives, exchange(): lax.all_to_all(blocks, axes, split_axis=0, concat_axis=0, tiled=False)  52.3 us
    all_to_all x2, starting transfers between devices, exchange(): lax.all_to_all(blocks, axes, split_axis=0, concat_axis=0, tiled=False)  24.2 us
    all_to_all x2, waiting for transfers between devices, exchange(): lax.all_to_all(blocks, axes, split_axis=0, concat_axis=0, tiled=False)  14.2 us
  transfers between devices with their start and end apart: 2, of which 2 were waited for; matrix products, arithmetic and copies ran while one was open for 3% of the time, Pallas kernels for 0%

profile of v1, /device:TPU:1, one launch (start us, length us, event | category | flops | bytes accessed | tf_op | source)
XLA Modules:
  0.0 118.8 jit_solution(15114217716822834184)
XLA Ops:
  0.6 0.7 broadcast_compare_fusion
  1.4 0.2 reduce-window.9
  1.6 1.3 %fusion.3 = (s32[]{:T(128)}, s32[]{:T(128)}, s32[]{:T(128)}, s32[4]{0:T(128)S(1)}) fusion(s32[4]{0:T(128)} %param.13, s32[4,1]{0,1:T(1,128)S(1)} %reduce-window.9), kind=kLoop, calls=%fused_computation.37 | loop fusion | flops 61 | bytes 60 | tf_op jit(solution)/shard_map/reduce_sum | solution.py:38
  8.7 1.3 %constant_dynamic-slice_fusion.6 = (bf16[1,1,192,640]{3,2,1,0:T(8,128)(2,1)S(1)}, bf16[1,1,192,640]{3,2,1,0:T(8,128)(2,1)S(1)}, bf16[1,1,192,640]{3,2,1,0:T(8,128)(2,1)S(1)}) fusion(bf16[1,4,192,640]{3,2,1,0:T(8,128)(2,1)} %param.8, s32[]{:T(128)S(6)} %select_n.38, s32[]{:T(128)S(6)} %select_n.42, s32[]{:T(128)S(6)} %select_n.40), kind=kLoop, calls=%fused_computation.26 | loop fusion | bytes 1474572 | tf_op jit(solution)/shard_map/jit(dynamic_index_in_dim)/dynamic_slice | solution.py:40
  10.0 0.3 maximum_bitcast_fusion
  10.3 0.1 copy.105
  10.4 25.8 %all_to_all.25 = bf16[8,7,24,640]{3,2,1,0:T(8,128)(2,1)S(1)} all-to-all(bf16[8,7,24,640]{3,2,1,0:T(8,128)(2,1)S(1)} %copy.105), channel_id=1, replica_groups=mesh['zl'=2,'x'=4,'y'=8,'zh'=4,'core'=2] {'zl','x'}, dimensions={0} | all-to-all | bytes 3440640 | tf_op jit(solution)/shard_map/all_to_all | solution.py:21
  36.3 0.2 convert_reduce_fusion
  36.5 0.1 copy.107
  36.8 0.9 copy.109
  37.6 9.2 %all-to-all-start.1 = ((f32[8,21,640]{2,1,0:T(8,128)}), f32[8,21,640]{2,1,0:T(8,128)S(1)}, u32[]{:S(2)}, u32[]{:S(2)}) async-start(f32[8,21,640]{2,1,0:T(8,128)} %copy.109), calls=%async_computation.1 | async-start | bytes 983040 | tf_op jit(solution)/shard_map/all_to_all | solution.py:21
  46.9 0.6 fusion.9
  50.8 10.2 %all-to-all-done.1 = f32[8,21,640]{2,1,0:T(8,128)S(1)} async-done(((f32[8,21,640]{2,1,0:T(8,128)}), f32[8,21,640]{2,1,0:T(8,128)S(1)}, u32[]{:S(2)}, u32[]{:S(2)}) %all-to-all-start.1) | async-done | bytes 430112 | tf_op jit(solution)/shard_map/all_to_all | solution.py:21
  61.1 0.7 convert_reduce_fusion.1
  63.4 11.8 %all_to_all.26 = bf16[8,16,640]{2,1,0:T(8,128)(2,1)S(1)} all-to-all(bf16[8,16,640]{2,1,0:T(8,128)(2,1)S(1)} %broadcast_in_dim.24), channel_id=1, replica_groups=mesh['zl'=2,'x'=4,'y'=8,'zh'=4,'core'=2] {'y'}, dimensions={0} | all-to-all | bytes 327680 | tf_op jit(solution)/shard_map/all_to_all | solution.py:21
  75.1 0.1 copy.125
  75.2 0.6 add_reduce_fusion.1
  77.3 0.1 reshape.294
  77.4 0.1 stack.20
  77.6 0.1 pad_maximum_fusion
  77.7 0.1 broadcast_in_dim.44
  77.8 14.7 %all_to_all.27 = bf16[8,112,640]{2,1,0:T(8,128)(2,1)S(1)} all-to-all(bf16[8,112,640]{2,1,0:T(8,128)(2,1)S(1)} %broadcast_in_dim.44), channel_id=1, replica_groups=mesh['zl'=2,'x'=4,'y'=8,'zh'=4,'core'=2] {'zl','x'}, dimensions={0} | all-to-all | bytes 2293760 | tf_op jit(solution)/shard_map/all_to_all | solution.py:21
  92.5 0.1 copy.126
  92.6 0.6 add_reduce_fusion
  93.2 1.2 %broadcast_in_dim.45 = f32[8,1,128]{2,1,0:T(1,128)} broadcast(f32[]{:T(128)} %add_reduce_fusion), dimensions={} | broadcast | bytes 4100 | tf_op jit(solution)/shard_map/broadcast_in_dim | solution.py:88
  94.5 14.9 %all-to-all-start.4 = ((f32[8,1,128]{2,1,0:T(1,128)}), f32[8,1,128]{2,1,0:T(1,128)S(1)}, u32[]{:S(2)}, u32[]{:S(2)}) async-start(f32[8,1,128]{2,1,0:T(1,128)} %broadcast_in_dim.45), calls=%async_computation.4 | async-start | bytes 8192 | tf_op jit(solution)/shard_map/all_to_all | solution.py:21
  109.4 0.6 copy.121
  110.0 0.6 copy.119
  110.7 0.6 copy.120
  111.4 1.0 copy.116
  112.4 4.0 %all-to-all-done.4 = f32[8,1,128]{2,1,0:T(1,128)S(1)} async-done(((f32[8,1,128]{2,1,0:T(1,128)}), f32[8,1,128]{2,1,0:T(1,128)S(1)}, u32[]{:S(2)}, u32[]{:S(2)}) %all-to-all-start.4) | async-done | bytes 4128 | tf_op jit(solution)/shard_map/all_to_all | solution.py:21
  116.4 0.6 slice_reduce_fusion
  (27 shorter events, 0.7 us)
Async XLA Ops:
  0.6 9.3 %copy-start = (bf16[1,4,192,640]{3,2,1,0:T(8,128)(2,1)S(1)}, bf16[1,4,192,640]{3,2,1,0:T(8,128)(2,1)}, u32[]{:S(2)}) copy-start(bf16[1,4,192,640]{3,2,1,0:T(8,128)(2,1)} %param.7) | copy-start | bytes 2949124
  36.6 24.4 %copy-start.1 = (f32[4,3,640]{2,0,1:T(4,128)S(1)}, f32[4,3,640]{2,0,1:T(4,128)}, u32[]{:S(2)}) copy-start(f32[4,3,640]{2,0,1:T(4,128)} %param.10) | copy-start | bytes 92164
  36.6 24.4 %copy-start.2 = (f32[4,3,640]{2,0,1:T(4,128)S(1)}, f32[4,3,640]{2,0,1:T(4,128)}, u32[]{:S(2)}) copy-start(f32[4,3,640]{2,0,1:T(4,128)} %param.9) | copy-start | bytes 92164
  36.8 26.4 %copy-start.3 = (f32[4,3,640]{2,0,1:T(4,128)S(1)}, f32[4,3,640]{2,0,1:T(4,128)}, u32[]{:S(2)}) copy-start(f32[4,3,640]{2,0,1:T(4,128)} %param.11) | copy-start | bytes 92164
  37.6 23.3 %all-to-all-start.1 = ((f32[8,21,640]{2,1,0:T(8,128)}), f32[8,21,640]{2,1,0:T(8,128)S(1)}, u32[]{:S(2)}, u32[]{:S(2)}) async-start(f32[8,21,640]{2,1,0:T(8,128)} %copy.109), calls=%async_computation.1 | async-start | bytes 983040 | tf_op jit(solution)/shard_map/all_to_all | solution.py:21
  94.5 21.9 %all-to-all-start.4 = ((f32[8,1,128]{2,1,0:T(1,128)}), f32[8,1,128]{2,1,0:T(1,128)S(1)}, u32[]{:S(2)}, u32[]{:S(2)}) async-start(f32[8,1,128]{2,1,0:T(1,128)} %broadcast_in_dim.45), calls=%async_computation.4 | async-start | bytes 8192 | tf_op jit(solution)/shard_map/all_to_all | solution.py:21

commit v2 on v1

v2 whole, which is shorter than its diff:
```python
import jax
import jax.numpy as jnp
from jax import lax
from jax.sharding import Mesh
from jax.sharding import PartitionSpec as P

BETA_ONE = 0.965
BETA_TWO = 0.99
RHO_SCALE = 0.5
LEARN_RATE = 0.0006
DECAY_RATE = 0.1

ZL, X, Y, ZH, CORE = 2, 4, 8, 4, 2
DP = ("zl", "x", "y")
TENSOR = ("zh", "core")
FIRST = ("zl", "x")
LIFT = 256.0


def exchange(blocks, axes):
    return lax.all_to_all(blocks, axes, split_axis=0, concat_axis=0, tiled=False)


def encode(v):
    w = v * LIFT
    w2 = w * w
    w4 = w2 * w2
    w8 = w4 * w4
    return jnp.where(v < 0.0, -w8, w8).astype(jnp.bfloat16)


def decode(code):
    t = code.astype(jnp.float32)
    size = jnp.sqrt(jnp.sqrt(jnp.sqrt(jnp.abs(t)))) * (1.0 / LIFT)
    return jnp.where(t < 0.0, -size, size)


def local(grad_part, hess_part, momentum, hessian, master, step, refresh):
    layers, rows, cols = grad_part.shape[1:]
    outer, inner = ZL * X, Y
    block, own = rows // outer, rows // (outer * inner)
    slots = layers - 1
    lots = layers + slots

    idle = [jnp.reshape(refresh[l : l + 1] <= 0, (1, 1, 1)) for l in range(layers)]
    past = [idle[0]]
    for l in range(1, slots):
        past.append(past[-1] | idle[l])
    grad, hess = grad_part[0], hess_part[0]
    chosen = [jnp.where(past[s], hess[s + 1 : s + 2], hess[s : s + 1]) for s in range(slots)]
    stacked = jnp.concatenate([grad] + chosen, axis=0)
    blocks = stacked.reshape(lots, outer, block, cols).transpose(1, 0, 2, 3)

    came = exchange(blocks, FIRST)
    partial = jnp.sum(came.astype(jnp.float32), axis=0)
    partial = partial.reshape(lots, inner, own, cols).transpose(1, 0, 2, 3)
    came = exchange(encode(partial).reshape(inner, lots * own, cols), "y")
    sums = jnp.sum(decode(came), axis=0).reshape(lots, own, cols)
    grad_sum = sums[:layers]
    held = [sums[layers + s : layers + s + 1] for s in range(slots)]
    hess_sum = jnp.concatenate(
        [held[0]]
        + [jnp.where(past[l - 1], held[l - 1], held[l]) for l in range(1, slots)]
        + [held[slots - 1]],
        axis=0,
    )

    new_momentum = BETA_ONE * momentum + (1.0 - BETA_ONE) * grad_sum
    layer_flags = (refresh > 0)[:, None, None]
    new_hessian = jnp.where(layer_flags, BETA_TWO * hessian + (1.0 - BETA_TWO) * hess_sum, hessian)
    correction = 1.0 - jnp.power(jnp.float32(BETA_ONE), step.astype(jnp.float32))
    ratios = new_momentum / jnp.reshape(correction, (1, 1, 1)) / (RHO_SCALE * new_hessian)
    clipped = jnp.clip(ratios, -1.0, 1.0)
    new_master = master * (1.0 - LEARN_RATE * DECAY_RATE) - LEARN_RATE * clipped
    mine = new_master.astype(jnp.bfloat16)
    count = jnp.sum((jnp.abs(ratios) >= 1.0).astype(jnp.float32), axis=(0, 1))[None]

    load = jnp.concatenate([mine.reshape(layers * own, cols), count.astype(jnp.bfloat16)], axis=0)
    load = jnp.pad(load, ((0, 3), (0, 0)))
    came = exchange(jnp.broadcast_to(load[None], (inner,) + load.shape), "y")
    held = came[:, : layers * own].reshape(inner, layers, own, cols).transpose(1, 0, 2, 3)
    held = held.reshape(layers * block, cols)
    count = jnp.sum(came[:, layers * own].astype(jnp.float32), axis=0)[None]

    load = jnp.concatenate([held, count.astype(jnp.bfloat16)], axis=0)
    load = jnp.pad(load, ((0, 15), (0, 0)))
    came = exchange(jnp.broadcast_to(load[None], (outer,) + load.shape), FIRST)
    weights = came[:, : layers * block].reshape(outer, layers, block, cols).transpose(1, 0, 2, 3)
    weights = weights.reshape(layers, rows, cols)
    count = jnp.sum(came[:, layers * block].astype(jnp.float32), axis=0)

    count = jnp.sum(count.reshape(cols // 128, 128), axis=0)
    came = exchange(jnp.broadcast_to(count[None, None], (ZH * CORE, 1, 128)), TENSOR)
    total = jnp.sum(came)
    entries = ratios.size * outer * inner * ZH * CORE
    clip_fraction = jnp.reshape(total / entries, (1,))
    return (new_momentum, new_hessian, new_master, weights, clip_fraction)


def solution(mesh):
    fine = Mesh(mesh.devices.reshape(ZL, X, Y, ZH, CORE), DP + TENSOR)
    shards = P(DP, None, None, TENSOR)
    state = P(None, DP, TENSOR)
    in_specs = (shards, shards, state, state, state, P(), P())
    out_specs = (state, state, state, P(None, None, TENSOR), P())
    return jax.shard_map(local, mesh=fine, in_specs=in_specs, out_specs=out_specs, check_vma=False)
```

time: 119 us -> 104 us (0.87)
  between operations: 14.4 us -> 5.31 us
  other arithmetic: 5.64 us -> 3.5 us
  local copies, waits for them, and re-layouts: 8.08 us -> 6.35 us
  waiting for transfers between devices: 14.2 us -> 12.5 us
  blocking collectives: 52.3 us -> 50.9 us
    reduce_sum x6, other arithmetic: 3.89 us -> 1.18 us  [the longest x1 0.6 us: local(): total = jnp.sum(came)]
    all_to_all x2, waiting for transfers between devices: 14.2 us -> 12.5 us  [exchange(): lax.all_to_all(blocks, axes, split_axis=0, concat_axis=0, tiled=False)]
    all_to_all x3, blocking collectives: 52.3 us -> 50.9 us  [exchange(): lax.all_to_all(blocks, axes, split_axis=0, concat_axis=0, tiled=False)]
    select_n x0 -> x1, other arithmetic: none -> 1.39 us  [local(): jnp.where(past[s], hess[s + 1:s + 2], hess[s:s + 1])]
    dynamic_slice x2 -> x0, local copies, waits for them, and re-layouts: 1.27 us -> none  [the longest x1 1.25 us: local(): lax.dynamic_index_in_dim(hess_part[0], p, 0, keepdims=True)]
where the time goes in v2:
time: 104 us; the launch traced here: 103 us
  blocking collectives  50.9 us (49%)
  starting transfers between devices  24.6 us (24%)
  waiting for transfers between devices  12.5 us (12%)
  local copies, waits for them, and re-layouts  6.35 us (6%)
  between operations  5.31 us (5%)
  other arithmetic  3.5 us (3%)
    all_to_all x3, blocking collectives, exchange(): lax.all_to_all(blocks, axes, split_axis=0, concat_axis=0, tiled=False)  50.9 us
    all_to_all x2, starting transfers between devices, exchange(): lax.all_to_all(blocks, axes, split_axis=0, concat_axis=0, tiled=False)  24.6 us
    all_to_all x2, waiting for transfers between devices, exchange(): lax.all_to_all(blocks, axes, split_axis=0, concat_axis=0, tiled=False)  12.5 us
  transfers between devices with their start and end apart: 2, of which 2 were waited for; matrix products, arithmetic and copies ran while one was open for 3% of the time, Pallas kernels for 0%

profile of v2, /device:TPU:1, one launch (start us, length us, event | category | flops | bytes accessed | tf_op | source)
XLA Modules:
  0.0 103.1 jit_solution(2516714241707569957)
XLA Ops:
  0.6 1.4 %fusion.19 = (s32[1]{0:T(128)}, s32[1]{0:T(128)}, s32[1]{0:T(128)}) fusion(s32[4]{0:T(128)} %param.13), kind=kLoop, calls=%fused_computation.47 | loop fusion | bytes 24 | tf_op jit(solution)/shard_map/slice | solution.py:45
  4.0 1.4 %slice_select_fusion.1 = (bf16[1,1,192,640]{3,2,1,0:T(8,128)(2,1)S(1)}, bf16[1,1,192,640]{3,2,1,0:T(8,128)(2,1)S(1)}, bf16[1,1,192,640]{3,2,1,0:T(8,128)(2,1)S(1)}) fusion(bf16[1,4,192,640]{3,2,1,0:T(8,128)(2,1)} %param.8, pred[]{:T(512)} %bitcast.1, pred[]{:T(512)} %bitcast.5, pred[]{:T(512)} %bitcast.3), kind=kLoop, calls=%fused_computation.17 | loop fusion | flops 368640 | bytes 1720323 | tf_op jit(solution)/shard_map/jit(_where)/select_n | solution.py:50
  5.4 0.3 maximum_bitcast_fusion
  5.7 0.1 copy.100
  5.8 25.8 %all_to_all.25 = bf16[8,7,24,640]{3,2,1,0:T(8,128)(2,1)S(1)} all-to-all(bf16[8,7,24,640]{3,2,1,0:T(8,128)(2,1)S(1)} %copy.100), channel_id=1, replica_groups=mesh['zl'=2,'x'=4,'y'=8,'zh'=4,'core'=2] {'zl','x'}, dimensions={0} | all-to-all | bytes 3440640 | tf_op jit(solution)/shard_map/all_to_all | solution.py:21
  31.7 0.2 convert_reduce_fusion
  31.9 0.1 multiply_multiply_fusion
  32.0 0.0 copy-start.4
  32.0 0.1 broadcast_compare_fusion
  32.1 0.0 copy-start.1
  32.1 0.1 copy.104
  32.2 0.1 copy.102
  32.3 0.1 fusion.5
  32.4 0.7 copy.106
  33.1 9.2 %all-to-all-start.1 = ((bf16[8,21,640]{2,1,0:T(8,128)(2,1)}), bf16[8,21,640]{2,1,0:T(8,128)(2,1)S(1)}, u32[]{:S(2)}, u32[]{:S(2)}) async-start(bf16[8,21,640]{2,1,0:T(8,128)(2,1)} %copy.106), calls=%async_computation.1 | async-start | bytes 491520 | tf_op jit(solution)/shard_map/all_to_all | solution.py:21
  43.1 8.5 %all-to-all-done.1 = bf16[8,21,640]{2,1,0:T(8,128)(2,1)S(1)} async-done(((bf16[8,21,640]{2,1,0:T(8,128)(2,1)}), bf16[8,21,640]{2,1,0:T(8,128)(2,1)S(1)}, u32[]{:S(2)}, u32[]{:S(2)}) %all-to-all-start.1) | async-done | bytes 215072 | tf_op jit(solution)/shard_map/all_to_all | solution.py:21
  51.6 0.5 fusion.4
  52.1 0.1 fusion.16
  52.3 10.8 %all_to_all.26 = bf16[8,16,640]{2,1,0:T(8,128)(2,1)S(1)} all-to-all(bf16[8,16,640]{2,1,0:T(8,128)(2,1)S(1)} %broadcast_in_dim.75), channel_id=1, replica_groups=mesh['zl'=2,'x'=4,'y'=8,'zh'=4,'core'=2] {'y'}, dimensions={0} | all-to-all | bytes 327680 | tf_op jit(solution)/shard_map/all_to_all | solution.py:21
  63.1 0.1 copy.111
  63.2 0.1 reshape.185
  63.4 0.1 broadcast_in_dim.76
  63.5 14.3 %all_to_all.27 = bf16[8,112,640]{2,1,0:T(8,128)(2,1)S(1)} all-to-all(bf16[8,112,640]{2,1,0:T(8,128)(2,1)S(1)} %broadcast_in_dim.76), channel_id=1, replica_groups=mesh['zl'=2,'x'=4,'y'=8,'zh'=4,'core'=2] {'zl','x'}, dimensions={0} | all-to-all | bytes 2293760 | tf_op jit(solution)/shard_map/all_to_all | solution.py:21
  77.8 0.6 broadcast_in_dim.77
  78.4 15.4 %all-to-all-start.4 = ((f32[8,1,128]{2,1,0:T(1,128)}), f32[8,1,128]{2,1,0:T(1,128)S(1)}, u32[]{:S(2)}, u32[]{:S(2)}) async-start(f32[8,1,128]{2,1,0:T(1,128)} %broadcast_in_dim.77), calls=%async_computation.4 | async-start | bytes 8192 | tf_op jit(solution)/shard_map/all_to_all | solution.py:21
  93.8 0.6 copy.114
  94.4 0.6 copy.115
  95.0 0.6 copy.116
  95.6 0.1 slice.82
  95.7 1.0 %copy.112 = bf16[4,8,24,640]{3,2,1,0:T(8,128)(2,1)} copy(bf16[4,8,24,640]{3,2,0,1:T(8,128)(2,1)S(1)} %bitcast.37) | data formatting | bytes 1966080 | tf_op jit(solution)/shard_map/transpose | solution.py:88
  96.8 4.0 %all-to-all-done.4 = f32[8,1,128]{2,1,0:T(1,128)S(1)} async-done(((f32[8,1,128]{2,1,0:T(1,128)}), f32[8,1,128]{2,1,0:T(1,128)S(1)}, u32[]{:S(2)}, u32[]{:S(2)}) %all-to-all-start.4) | async-done | bytes 4128 | tf_op jit(solution)/shard_map/all_to_all | solution.py:21
  100.8 0.6 reduce_sum.72
  (23 shorter events, 0.3 us)
Async XLA Ops:
  0.6 4.7 %copy-start = (bf16[1,4,192,640]{3,2,1,0:T(8,128)(2,1)S(1)}, bf16[1,4,192,640]{3,2,1,0:T(8,128)(2,1)}, u32[]{:S(2)}) copy-start(bf16[1,4,192,640]{3,2,1,0:T(8,128)(2,1)} %param.7) | copy-start | bytes 2949124
  32.0 11.1 %copy-start.4 = (s32[4]{0:T(128)S(1)}, s32[4]{0:T(128)}, u32[]{:S(2)}) copy-start(s32[4]{0:T(128)} %param.13) | copy-start | bytes 52
  32.1 20.0 %copy-start.1 = (f32[4,3,640]{2,0,1:T(4,128)S(1)}, f32[4,3,640]{2,0,1:T(4,128)}, u32[]{:S(2)}) copy-start(f32[4,3,640]{2,0,1:T(4,128)} %param.11) | copy-start | bytes 92164
  32.1 20.0 %copy-start.2 = (f32[4,3,640]{2,0,1:T(4,128)S(1)}, f32[4,3,640]{2,0,1:T(4,128)}, u32[]{:S(2)}) copy-start(f32[4,3,640]{2,0,1:T(4,128)} %param.10) | copy-start | bytes 92164
  32.1 20.0 %copy-start.3 = (f32[4,3,640]{2,0,1:T(4,128)S(1)}, f32[4,3,640]{2,0,1:T(4,128)}, u32[]{:S(2)}) copy-start(f32[4,3,640]{2,0,1:T(4,128)} %param.9) | copy-start | bytes 92164
  33.1 18.5 %all-to-all-start.1 = ((bf16[8,21,640]{2,1,0:T(8,128)(2,1)}), bf16[8,21,640]{2,1,0:T(8,128)(2,1)S(1)}, u32[]{:S(2)}, u32[]{:S(2)}) async-start(bf16[8,21,640]{2,1,0:T(8,128)(2,1)} %copy.106), calls=%async_computation.1 | async-start | bytes 491520 | tf_op jit(solution)/shard_map/all_to_all | solution.py:21
  78.4 22.4 %all-to-all-start.4 = ((f32[8,1,128]{2,1,0:T(1,128)}), f32[8,1,128]{2,1,0:T(1,128)S(1)}, u32[]{:S(2)}, u32[]{:S(2)}) async-start(f32[8,1,128]{2,1,0:T(1,128)} %broadcast_in_dim.77), calls=%async_computation.4 | async-start | bytes 8192 | tf_op jit(solution)/shard_map/all_to_all | solution.py:21

commit v3 on v2

--- a/solution.py
+++ b/solution.py
@@ -1,6 +1,8 @@
 import jax
 import jax.numpy as jnp
 from jax import lax
+from jax.experimental import pallas as pl
+from jax.experimental.pallas import tpu as pltpu
 from jax.sharding import Mesh
 from jax.sharding import PartitionSpec as P
 
@@ -35,6 +37,42 @@
     return jnp.where(t < 0.0, -size, size)
 
 
+def pack_kernel(refresh, grad, hess, blocks, flags, flag_sem, sems):
+    layers = grad.shape[0]
+    read = pltpu.make_async_copy(refresh, flags, flag_sem)
+    read.start()
+    copies = [pltpu.make_async_copy(grad.at[l], blocks.at[:, l], sems.at[l]) for l in range(layers)]
+    for copy in copies:
+        copy.start()
+    read.wait()
+    past = jnp.int32(0)
+    for s in range(layers - 1):
+        past = jnp.where(flags[s] > 0, past, 1)
+        copy = pltpu.make_async_copy(hess.at[s + past], blocks.at[:, layers + s], sems.at[layers + s])
+        copy.start()
+        copies.append(copy)
+    for copy in copies:
+        copy.wait()
+
+
+def pack(refresh, grad, hess):
+    layers, outer, block, cols = grad.shape
+    lots = 2 * layers - 1
+    return pl.pallas_call(
+        pack_kernel,
+        out_shape=pltpu.VMEM((outer, lots, block, cols), grad.dtype),
+        in_specs=[pl.BlockSpec(memory_space=pl.ANY)] * 3,
+        out_specs=pl.BlockSpec(memory_space=pl.ANY),
+        scratch_shapes=[
+            pltpu.SMEM((layers,), jnp.int32),
+            pltpu.SemaphoreType.DMA,
+            pltpu.SemaphoreType.DMA((lots,)),
+        ],
+        compiler_params=pltpu.CompilerParams(vmem_limit_bytes=8 * 1024 * 1024),
+        name="pack",
+    )(*(pltpu.with_memory_space_constraint(a, pltpu.HBM) for a in (refresh, grad, hess)))
+
+
 def local(grad_part, hess_part, momentum, hessian, master, step, refresh):
     layers, rows, cols = grad_part.shape[1:]
     outer, inner = ZL * X, Y
@@ -46,10 +84,8 @@
     past = [idle[0]]
     for l in range(1, slots):
         past.append(past[-1] | idle[l])
-    grad, hess = grad_part[0], hess_part[0]
-    chosen = [jnp.where(past[s], hess[s + 1 : s + 2], hess[s : s + 1]) for s in range(slots)]
-    stacked = jnp.concatenate([grad] + chosen, axis=0)
-    blocks = stacked.reshape(lots, outer, block, cols).transpose(1, 0, 2, 3)
+    shape = (layers, outer, block, cols)
+    blocks = pack(refresh, grad_part.reshape(shape), hess_part.reshape(shape))
 
     came = exchange(blocks, FIRST)
     partial = jnp.sum(came.astype(jnp.float32), axis=0)
@@ -83,7 +119,6 @@
     count = jnp.sum(came[:, layers * own].astype(jnp.float32), axis=0)[None]
 
     load = jnp.concatenate([held, count.astype(jnp.bfloat16)], axis=0)
-    load = jnp.pad(load, ((0, 15), (0, 0)))
     came = exchange(jnp.broadcast_to(load[None], (outer,) + load.shape), FIRST)
     weights = came[:, : layers * block].reshape(outer, layers, block, cols).transpose(1, 0, 2, 3)
     weights = weights.reshape(layers, rows, cols)

time: 104 us -> 99.8 us (0.960)
  Pallas kernels: 0 us -> 2.07 us
  waiting for transfers between devices: 12.5 us -> 10.6 us
  other arithmetic: 3.5 us -> 1.82 us
    pallas_call x0 -> x1, Pallas kernels: none -> 2.07 us  [pack(): pl.pallas_call(pack_kernel, out_shape=pltpu.VMEM((outer, lots, block, col...]
    all_to_all x2, waiting for transfers between devices: 12.5 us -> 10.6 us  [exchange(): lax.all_to_all(blocks, axes, split_axis=0, concat_axis=0, tiled=False)]
    select_n x1 -> x0, other arithmetic: 1.39 us -> none  [local(): jnp.where(past[s], hess[s + 1:s + 2], hess[s:s + 1])]
  transfers between devices with their start and end apart: 2 -> 2, of which waited for: 2 -> 2; matrix products, arithmetic and copies ran while one was open for 3% -> 4% of each run, Pallas kernels for 0% -> 0%
where the time goes in v3:
time: 99.8 us; the launch traced here: 99.4 us
  blocking collectives  50.2 us (50%)
  starting transfers between devices  24.7 us (25%)
  waiting for transfers between devices  10.6 us (11%)
  local copies, waits for them, and re-layouts  5.41 us (5%)
  between operations  4.62 us (5%)
  Pallas kernels  2.07 us (2%)
  other arithmetic  1.82 us (2%)
    all_to_all x3, blocking collectives, exchange(): lax.all_to_all(blocks, axes, split_axis=0, concat_axis=0, tiled=False)  50.2 us
    all_to_all x2, starting transfers between devices, exchange(): lax.all_to_all(blocks, axes, split_axis=0, concat_axis=0, tiled=False)  24.7 us
    all_to_all x2, waiting for transfers between devices, exchange(): lax.all_to_all(blocks, axes, split_axis=0, concat_axis=0, tiled=False)  10.6 us
    pallas_call x1, Pallas kernels, pack(): pl.pallas_call(pack_kernel, out_shape=pltpu.VMEM((outer, lots, block, col...  2.07 us
  transfers between devices with their start and end apart: 2, of which 2 were waited for; matrix products, arithmetic and copies ran while one was open for 4% of the time, Pallas kernels for 0%

profile of v3, /device:TPU:1, one launch (start us, length us, event | category | flops | bytes accessed | tf_op | source)
XLA Modules:
  0.0 99.4 jit_solution(1118561144449309638)
XLA Ops:
  0.6 2.1 %pack.1 = bf16[8,7,24,640]{3,2,1,0:T(8,128)(2,1)S(1)} custom-call(s32[4]{0:T(128)} %refresh.1, bf16[4,8,24,640]{3,2,1,0:T(8,128)(2,1)} %bitcast.35, bf16[4,8,24,640]{3,2,1,0:T(8,128)(2,1)} %bitcast.36), custom_call_target="tpu_custom_call" | custom-call | tf_op jit(solution)/shard_map/pack/pallas_call | solution.py:61
  2.7 25.8 %all_to_all.25 = bf16[8,7,24,640]{3,2,1,0:T(8,128)(2,1)S(1)} all-to-all(bf16[8,7,24,640]{3,2,1,0:T(8,128)(2,1)S(1)} %pack.1), channel_id=1, replica_groups=mesh['zl'=2,'x'=4,'y'=8,'zh'=4,'core'=2] {'zl','x'}, dimensions={0} | all-to-all | bytes 3440640 | tf_op jit(solution)/shard_map/all_to_all | solution.py:23
  28.6 0.2 convert_reduce_fusion
  28.8 0.1 multiply_multiply_fusion
  28.9 0.0 copy-start.3
  28.9 0.1 broadcast_compare_fusion
  29.0 0.0 copy-start
  29.0 0.0 copy-start.1
  29.0 0.0 copy-start.2
  29.0 0.1 copy.81
  29.1 0.1 copy.79
  29.2 0.1 fusion.5
  29.3 0.7 copy.83
  30.0 9.2 %all-to-all-start.1 = ((bf16[8,21,640]{2,1,0:T(8,128)(2,1)}), bf16[8,21,640]{2,1,0:T(8,128)(2,1)S(1)}, u32[]{:S(2)}, u32[]{:S(2)}) async-start(bf16[8,21,640]{2,1,0:T(8,128)(2,1)} %copy.83), calls=%async_computation.1 | async-start | bytes 491520 | tf_op jit(solution)/shard_map/all_to_all | solution.py:23
  39.2 0.6 fusion.16
  41.8 6.6 %all-to-all-done.1 = bf16[8,21,640]{2,1,0:T(8,128)(2,1)S(1)} async-done(((bf16[8,21,640]{2,1,0:T(8,128)(2,1)}), bf16[8,21,640]{2,1,0:T(8,128)(2,1)S(1)}, u32[]{:S(2)}, u32[]{:S(2)}) %all-to-all-start.1) | async-done | bytes 215072 | tf_op jit(solution)/shard_map/all_to_all | solution.py:23
  48.5 0.5 fusion.4
  49.0 0.1 fusion.13
  49.2 10.8 %all_to_all.26 = bf16[8,16,640]{2,1,0:T(8,128)(2,1)S(1)} all-to-all(bf16[8,16,640]{2,1,0:T(8,128)(2,1)S(1)} %broadcast_in_dim.51), channel_id=1, replica_groups=mesh['zl'=2,'x'=4,'y'=8,'zh'=4,'core'=2] {'y'}, dimensions={0} | all-to-all | bytes 327680 | tf_op jit(solution)/shard_map/all_to_all | solution.py:23
  60.0 0.1 copy.88
  60.1 0.1 reshape.103
  60.3 0.1 broadcast_in_dim.52
  60.4 13.5 %all_to_all.27 = bf16[8,97,640]{2,1,0:T(8,128)(2,1)S(1)} all-to-all(bf16[8,97,640]{2,1,0:T(8,128)(2,1)S(1)} %broadcast_in_dim.52), channel_id=1, replica_groups=mesh['zl'=2,'x'=4,'y'=8,'zh'=4,'core'=2] {'zl','x'}, dimensions={0} | all-to-all | bytes 1986560 | tf_op jit(solution)/shard_map/all_to_all | solution.py:23
  74.0 0.6 broadcast_in_dim.53
  74.6 15.4 %all-to-all-start.4 = ((f32[8,1,128]{2,1,0:T(1,128)}), f32[8,1,128]{2,1,0:T(1,128)S(1)}, u32[]{:S(2)}, u32[]{:S(2)}) async-start(f32[8,1,128]{2,1,0:T(1,128)} %broadcast_in_dim.53), calls=%async_computation.4 | async-start | bytes 8192 | tf_op jit(solution)/shard_map/all_to_all | solution.py:23
  90.0 0.6 copy.91
  90.6 0.6 copy.92
  91.3 0.6 copy.93
  91.9 0.1 slice.56
  92.0 1.0 %copy.89 = bf16[4,8,24,640]{3,2,1,0:T(8,128)(2,1)} copy(bf16[4,8,24,640]{3,2,0,1:T(8,128)(2,1)S(1)} %bitcast.32) | data formatting | bytes 1966080 | tf_op jit(solution)/shard_map/transpose | solution.py:123
  93.0 4.0 %all-to-all-done.4 = f32[8,1,128]{2,1,0:T(1,128)S(1)} async-done(((f32[8,1,128]{2,1,0:T(1,128)}), f32[8,1,128]{2,1,0:T(1,128)S(1)}, u32[]{:S(2)}, u32[]{:S(2)}) %all-to-all-start.4) | async-done | bytes 4128 | tf_op jit(solution)/shard_map/all_to_all | solution.py:23
  97.0 0.6 reduce_sum.72
  (19 shorter events, 0.3 us)
Async XLA Ops:
  28.9 10.4 %copy-start.3 = (s32[4]{0:T(128)S(1)}, s32[4]{0:T(128)}, u32[]{:S(2)}) copy-start(s32[4]{0:T(128)} %refresh.1) | copy-start | bytes 52
  29.0 20.0 %copy-start = (f32[4,3,640]{2,0,1:T(4,128)S(1)}, f32[4,3,640]{2,0,1:T(4,128)}, u32[]{:S(2)}) copy-start(f32[4,3,640]{2,0,1:T(4,128)} %param.11) | copy-start | bytes 92164
  29.0 20.0 %copy-start.1 = (f32[4,3,640]{2,0,1:T(4,128)S(1)}, f32[4,3,640]{2,0,1:T(4,128)}, u32[]{:S(2)}) copy-start(f32[4,3,640]{2,0,1:T(4,128)} %param.10) | copy-start | bytes 92164
  29.0 20.0 %copy-start.2 = (f32[4,3,640]{2,0,1:T(4,128)S(1)}, f32[4,3,640]{2,0,1:T(4,128)}, u32[]{:S(2)}) copy-start(f32[4,3,640]{2,0,1:T(4,128)} %param.9) | copy-start | bytes 92164
  30.0 18.5 %all-to-all-start.1 = ((bf16[8,21,640]{2,1,0:T(8,128)(2,1)}), bf16[8,21,640]{2,1,0:T(8,128)(2,1)S(1)}, u32[]{:S(2)}, u32[]{:S(2)}) async-start(bf16[8,21,640]{2,1,0:T(8,128)(2,1)} %copy.83), calls=%async_computation.1 | async-start | bytes 491520 | tf_op jit(solution)/shard_map/all_to_all | solution.py:23
  74.6 22.4 %all-to-all-start.4 = ((f32[8,1,128]{2,1,0:T(1,128)}), f32[8,1,128]{2,1,0:T(1,128)S(1)}, u32[]{:S(2)}, u32[]{:S(2)}) async-start(f32[8,1,128]{2,1,0:T(1,128)} %broadcast_in_dim.53), calls=%async_computation.4 | async-start | bytes 8192 | tf_op jit(solution)/shard_map/all_to_all | solution.py:23

commit v4 on v3

--- a/solution.py
+++ b/solution.py
@@ -1,3 +1,5 @@
+import functools
+
 import jax
 import jax.numpy as jnp
 from jax import lax
@@ -28,7 +30,7 @@
     w2 = w * w
     w4 = w2 * w2
     w8 = w4 * w4
-    return jnp.where(v < 0.0, -w8, w8).astype(jnp.bfloat16)
+    return jnp.where(v < 0.0, -w8, w8)
 
 
 def decode(code):
@@ -37,7 +39,7 @@
     return jnp.where(t < 0.0, -size, size)
 
 
-def pack_kernel(refresh, grad, hess, blocks, flags, flag_sem, sems):
+def pack_kernel(slots, refresh, grad, hess, blocks, marks, flags, flag_sem, sems):
     layers = grad.shape[0]
     read = pltpu.make_async_copy(refresh, flags, flag_sem)
     read.start()
@@ -45,24 +47,36 @@
     for copy in copies:
         copy.start()
     read.wait()
-    past = jnp.int32(0)
-    for s in range(layers - 1):
-        past = jnp.where(flags[s] > 0, past, 1)
-        copy = pltpu.make_async_copy(hess.at[s + past], blocks.at[:, layers + s], sems.at[layers + s])
+    ranks, rank = [], jnp.int32(0)
+    picks = [jnp.int32(0)] * slots
+    for l in range(layers):
+        used = flags[l] > 0
+        picks = [jnp.where(used & (rank == s), l, picks[s]) for s in range(slots)]
+        ranks.append(rank)
+        rank = rank + used.astype(jnp.int32)
+    for s in range(slots):
+        copy = pltpu.make_async_copy(hess.at[picks[s]], blocks.at[:, layers + s], sems.at[layers + s])
         copy.start()
         copies.append(copy)
+    for l in range(layers):
+        flag = (flags[l] > 0).astype(jnp.float32)
+        marks[l : l + 1] = jnp.full((1, marks.shape[1]), ranks[l].astype(jnp.float32))
+        marks[layers + l : layers + l + 1] = jnp.full((1, marks.shape[1]), flag)
     for copy in copies:
         copy.wait()
 
 
-def pack(refresh, grad, hess):
+def pack(slots, refresh, grad, hess):
     layers, outer, block, cols = grad.shape
-    lots = 2 * layers - 1
+    lots = layers + slots
     return pl.pallas_call(
-        pack_kernel,
-        out_shape=pltpu.VMEM((outer, lots, block, cols), grad.dtype),
+        functools.partial(pack_kernel, slots),
+        out_shape=(
+            pltpu.VMEM((outer, lots, block, cols), grad.dtype),
+            pltpu.VMEM((2 * layers, cols), jnp.float32),
+        ),
         in_specs=[pl.BlockSpec(memory_space=pl.ANY)] * 3,
-        out_specs=pl.BlockSpec(memory_space=pl.ANY),
+        out_specs=(pl.BlockSpec(memory_space=pl.ANY), pl.BlockSpec(memory_space=pltpu.VMEM)),
         scratch_shapes=[
             pltpu.SMEM((layers,), jnp.int32),
             pltpu.SemaphoreType.DMA,
@@ -73,36 +87,91 @@
     )(*(pltpu.with_memory_space_constraint(a, pltpu.HBM) for a in (refresh, grad, hess)))
 
 
+def fold_kernel(own, came, codes, rows):
+    outer, lots, block, _ = came.shape
+    for lot in range(lots):
+        total = came[0, lot].astype(jnp.float32)
+        for k in range(1, outer):
+            total += came[k, lot].astype(jnp.float32)
+        code = encode(total)
+        for y in range(block // own):
+            rows[y, lot * own : (lot + 1) * own] = code[y * own : (y + 1) * own]
+    codes[...] = rows[...].astype(codes.dtype)
+
+
+def fold(came):
+    _, lots, block, cols = came.shape
+    own = block // Y
+    shape = (Y, lots * own, cols)
+    return pl.pallas_call(
+        functools.partial(fold_kernel, own),
+        out_shape=pltpu.VMEM(shape, came.dtype),
+        in_specs=[pl.BlockSpec(memory_space=pltpu.VMEM)],
+        out_specs=pl.BlockSpec(memory_space=pltpu.VMEM),
+        scratch_shapes=[pltpu.VMEM(shape, jnp.float32)],
+        compiler_params=pltpu.CompilerParams(vmem_limit_bytes=16 * 1024 * 1024),
+        name="fold",
+    )(pltpu.with_memory_space_constraint(came, pltpu.VMEM))
+
+
+def reduce(slots, grad_part, hess_part, refresh):
+    layers, rows, cols = grad_part.shape[1:]
+    outer, inner = ZL * X, Y
+    block, own = rows // outer, rows // (outer * inner)
+    shape = (layers, outer, block, cols)
+    blocks, marks = pack(slots, refresh, grad_part.reshape(shape), hess_part.reshape(shape))
+    came = exchange(fold(exchange(blocks, FIRST)), "y")
+    sums = jnp.sum(decode(came), axis=0)
+    parts = [sums[: layers * own]]
+    held = [sums[(layers + s) * own : (layers + s + 1) * own] for s in range(slots)]
+    for l in range(layers):
+        mine = held[0]
+        for s in range(1, min(l + 1, slots)):
+            mine = jnp.where(marks[l : l + 1] >= s, held[s], mine)
+        parts.append(mine)
+    return jnp.concatenate(parts + [marks[layers:]], axis=0)
+
+
+def branch_kernel(refresh, index, flags, sem):
+    read = pltpu.make_async_copy(refresh, flags, sem)
+    read.start()
+    read.wait()
+    layers = refresh.shape[0]
+    count = jnp.int32(0)
+    for l in range(layers):
+        count = count + (flags[l] > 0).astype(jnp.int32)
+    index[0] = jnp.clip(count, 1, layers - 1) - 1
+
+
+def branch(refresh):
+    return pl.pallas_call(
+        branch_kernel,
+        out_shape=pltpu.SMEM((1,), jnp.int32),
+        in_specs=[pl.BlockSpec(memory_space=pl.ANY)],
+        out_specs=pl.BlockSpec(memory_space=pltpu.SMEM),
+        scratch_shapes=[pltpu.SMEM(refresh.shape, jnp.int32), pltpu.SemaphoreType.DMA],
+        compiler_params=pltpu.CompilerParams(vmem_limit_bytes=1024 * 1024),
+        name="branch",
+    )(pltpu.with_memory_space_constraint(refresh, pltpu.HBM))[0]
+
+
 def local(grad_part, hess_part, momentum, hessian, master, step, refresh):
     layers, rows, cols = grad_part.shape[1:]
     outer, inner = ZL * X, Y
     block, own = rows // outer, rows // (outer * inner)
-    slots = layers - 1
-    lots = layers + slots
-
-    idle = [jnp.reshape(refresh[l : l + 1] <= 0, (1, 1, 1)) for l in range(layers)]
-    past = [idle[0]]
-    for l in range(1, slots):
-        past.append(past[-1] | idle[l])
-    shape = (layers, outer, block, cols)
-    blocks = pack(refresh, grad_part.reshape(shape), hess_part.reshape(shape))
-
-    came = exchange(blocks, FIRST)
-    partial = jnp.sum(came.astype(jnp.float32), axis=0)
-    partial = partial.reshape(lots, inner, own, cols).transpose(1, 0, 2, 3)
-    came = exchange(encode(partial).reshape(inner, lots * own, cols), "y")
-    sums = jnp.sum(decode(came), axis=0).reshape(lots, own, cols)
-    grad_sum = sums[:layers]
-    held = [sums[layers + s : layers + s + 1] for s in range(slots)]
-    hess_sum = jnp.concatenate(
-        [held[0]]
-        + [jnp.where(past[l - 1], held[l - 1], held[l]) for l in range(1, slots)]
-        + [held[slots - 1]],
-        axis=0,
+
+    sums = lax.switch(
+        branch(refresh),
+        [functools.partial(reduce, slots) for slots in range(1, layers)],
+        grad_part,
+        hess_part,
+        refresh,
     )
+    grad_sum = sums[: layers * own].reshape(layers, own, cols)
+    hess_sum = sums[layers * own : 2 * layers * own].reshape(layers, own, cols)
+    layer_flags = sums[2 * layers * own :][:, None, :] > 0.0
 
     new_momentum = BETA_ONE * momentum + (1.0 - BETA_ONE) * grad_sum
-    layer_flags = (refresh > 0)[:, None, None]
     new_hessian = jnp.where(layer_flags, BETA_TWO * hessian + (1.0 - BETA_TWO) * hess_sum, hessian)
     correction = 1.0 - jnp.power(jnp.float32(BETA_ONE), step.astype(jnp.float32))
     ratios = new_momentum / jnp.reshape(correction, (1, 1, 1)) / (RHO_SCALE * new_hessian)
@@ -127,7 +196,7 @@
     count = jnp.sum(count.reshape(cols // 128, 128), axis=0)
     came = exchange(jnp.broadcast_to(count[None, None], (ZH * CORE, 1, 128)), TENSOR)
     total = jnp.sum(came)
-    entries = ratios.size * outer * inner * ZH * CORE
+    entries = layers * rows * cols * ZH * CORE
     clip_fraction = jnp.reshape(total / entries, (1,))
     return (new_momentum, new_hessian, new_master, weights, clip_fraction)
 

time: 99.8 us -> 98.6 us (0.988)
  waiting for transfers between devices: 10.6 us -> 13.2 us
  blocking collectives: 50.2 us -> 48.2 us
  Pallas kernels: 2.07 us -> 3.72 us
  between operations: 4.62 us -> 3.27 us
  local copies, waits for them, and re-layouts: 5.41 us -> 4.14 us
    all_to_all x2, waiting for transfers between devices: 10.6 us -> 13.2 us  [exchange(): lax.all_to_all(blocks, axes, split_axis=0, concat_axis=0, tiled=False)]
    all_to_all x3, blocking collectives: 50.2 us -> 48.2 us  [exchange(): lax.all_to_all(blocks, axes, split_axis=0, concat_axis=0, tiled=False)]
    pallas_call x1 -> x3, Pallas kernels: 2.07 us -> 3.72 us  [the longest x1 2 us: pack(): pl.pallas_call(functools.partial(pack_kernel, slots), out_shape=(pltpu.VM...]
  transfers between devices with their start and end apart: 2 -> 2, of which waited for: 2 -> 2; matrix products, arithmetic and copies ran while one was open for 4% -> 3% of each run, Pallas kernels for 0% -> 0%
where the time goes in v4:
time: 98.6 us; the launch traced here: 98.1 us
  blocking collectives  48.2 us (49%)
  starting transfers between devices  24.2 us (25%)
  waiting for transfers between devices  13.2 us (13%)
  local copies, waits for them, and re-layouts  4.14 us (4%)
  Pallas kernels  3.72 us (4%)
  between operations  3.27 us (3%)
  other arithmetic  1.36 us (1%)
    all_to_all x3, blocking collectives, exchange(): lax.all_to_all(blocks, axes, split_axis=0, concat_axis=0, tiled=False)  48.2 us
    all_to_all x2, starting transfers between devices, exchange(): lax.all_to_all(blocks, axes, split_axis=0, concat_axis=0, tiled=False)  24.2 us
    all_to_all x2, waiting for transfers between devices, exchange(): lax.all_to_all(blocks, axes, split_axis=0, concat_axis=0, tiled=False)  13.2 us
    pallas_call x1, Pallas kernels, pack(): pl.pallas_call(functools.partial(pack_kernel, slots), out_shape=(pltpu.VM...  2 us
  transfers between devices with their start and end apart: 2, of which 2 were waited for; matrix products, arithmetic and copies ran while one was open for 3% of the time, Pallas kernels for 0%

profile of v4, /device:TPU:1, one launch (start us, length us, event | category | flops | bytes accessed | tf_op | source)
XLA Modules:
  0.0 98.1 jit_solution(7347455730842537769)
XLA Ops:
  0.6 0.7 branch.1
  1.3 0.0 copy-start
  1.3 0.0 copy-start.1
  1.4 0.0 copy-start.2
  1.4 45.3 %conditional.1 = (f32[28,640]{1,0:T(8,128)S(1)}) conditional(s32[]{:T(128)} %bitcast.6, (bf16[1,4,192,640]{3,2,1,0:T(8,128)(2,1)}, bf16[1,4,192,640]{3,2,1,0:T(8,128)(2,1)}, s32[4]{0:T(128)}) %tuple.17, (bf16[1,4,192,640]{3,2,1,0:T(8,128)(2,1)}, bf16[1,4,192,640]{3,2,1,0:T(8,128)(2,1)}, s32[4]{0:T(128)}) %tuple.17, ...), branch_computations={%region_0.2_spmd, %region_2.4_spmd, %region_4.6_spmd} | conditional | flops 752000 | bytes 4716840 | solution.py:163
  1.4 2.0 %pack.4 = (bf16[8,6,24,640]{3,2,1,0:T(8,128)(2,1)S(1)}, f32[8,640]{1,0:T(8,128)S(1)}) custom-call(s32[4]{0:T(128)} %get-tuple-element.27.refresh, bf16[4,8,24,640]{3,2,1,0:T(8,128)(2,1)} %bitcast.21, bf16[4,8,24,640]{3,2,1,0:T(8,128)(2,1)} %bitcast.24), custom_call_target="tpu_custom_call" | custom-call | tf_op jit(solution)/shard_map/cond/branch_1_fun/pack/pallas_call | solution.py:72
  3.4 23.2 %all_to_all.40.came = bf16[8,6,24,640]{3,2,1,0:T(8,128)(2,1)S(1)} all-to-all(bf16[8,6,24,640]{3,2,1,0:T(8,128)(2,1)S(1)} %get-tuple-element.30), channel_id=1, replica_groups=mesh['zl'=2,'x'=4,'y'=8,'zh'=4,'core'=2] {'zl','x'}, dimensions={0} | all-to-all | bytes 2949120 | tf_op jit(solution)/shard_map/cond/branch_1_fun/all_to_all | solution.py:25
  26.6 1.0 %fold.4 = bf16[8,18,640]{2,1,0:T(8,128)(2,1)} custom-call(bf16[8,6,24,640]{3,2,1,0:T(8,128)(2,1)S(1)} %all_to_all.40.came), custom_call_target="tpu_custom_call" | custom-call | tf_op jit(solution)/shard_map/cond/branch_1_fun/fold/pallas_call | solution.py:106
  27.6 9.2 %all-to-all-start.3 = ((bf16[8,18,640]{2,1,0:T(8,128)(2,1)}), bf16[8,18,640]{2,1,0:T(8,128)(2,1)S(1)}, u32[]{:S(2)}, u32[]{:S(2)}) async-start(bf16[8,18,640]{2,1,0:T(8,128)(2,1)} %fold.4), calls=%async_computation.3 | async-start | bytes 491520 | tf_op jit(solution)/shard_map/cond/branch_1_fun/all_to_all | solution.py:25
  36.9 9.2 %all-to-all-done.3 = bf16[8,18,640]{2,1,0:T(8,128)(2,1)S(1)} async-done(((bf16[8,18,640]{2,1,0:T(8,128)(2,1)}), bf16[8,18,640]{2,1,0:T(8,128)(2,1)S(1)}, u32[]{:S(2)}, u32[]{:S(2)}) %all-to-all-start.3) | async-done | bytes 184352 | tf_op jit(solution)/shard_map/cond/branch_1_fun/all_to_all | solution.py:25
  46.0 0.5 fusion.9
  46.5 0.2 concatenate.14
  47.5 0.0 copy-done
  47.5 0.0 copy-done.1
  47.5 0.0 copy-done.2
  47.5 0.1 fusion.22
  47.7 10.8 %all_to_all.42 = bf16[8,16,640]{2,1,0:T(8,128)(2,1)S(1)} all-to-all(bf16[8,16,640]{2,1,0:T(8,128)(2,1)S(1)} %broadcast_in_dim.89), channel_id=1, replica_groups=mesh['zl'=2,'x'=4,'y'=8,'zh'=4,'core'=2] {'y'}, dimensions={0} | all-to-all | bytes 327680 | tf_op jit(solution)/shard_map/all_to_all | solution.py:25
  58.5 0.1 copy.60
  58.6 0.1 reshape.94
  58.7 0.1 broadcast_in_dim.90
  58.8 14.3 %all_to_all.43 = bf16[8,97,640]{2,1,0:T(8,128)(2,1)S(1)} all-to-all(bf16[8,97,640]{2,1,0:T(8,128)(2,1)S(1)} %broadcast_in_dim.90), channel_id=1, replica_groups=mesh['zl'=2,'x'=4,'y'=8,'zh'=4,'core'=2] {'zl','x'}, dimensions={0} | all-to-all | bytes 1986560 | tf_op jit(solution)/shard_map/all_to_all | solution.py:25
  73.2 0.6 broadcast_in_dim.91
  73.8 15.0 %all-to-all-start.8 = ((f32[8,1,128]{2,1,0:T(1,128)}), f32[8,1,128]{2,1,0:T(1,128)S(1)}, u32[]{:S(2)}, u32[]{:S(2)}) async-start(f32[8,1,128]{2,1,0:T(1,128)} %broadcast_in_dim.91), calls=%async_computation.8 | async-start | bytes 8192 | tf_op jit(solution)/shard_map/all_to_all | solution.py:25
  88.8 0.6 copy.65
  89.4 0.6 copy.64
  90.0 0.6 copy.63
  90.6 0.1 slice.98
  90.7 1.0 %copy.61 = bf16[4,8,24,640]{3,2,1,0:T(8,128)(2,1)} copy(bf16[4,8,24,640]{3,2,0,1:T(8,128)(2,1)S(1)} %bitcast.26) | data formatting | bytes 1966080 | tf_op jit(solution)/shard_map/transpose | solution.py:192
  91.8 4.0 %all-to-all-done.8 = f32[8,1,128]{2,1,0:T(1,128)S(1)} async-done(((f32[8,1,128]{2,1,0:T(1,128)}), f32[8,1,128]{2,1,0:T(1,128)S(1)}, u32[]{:S(2)}, u32[]{:S(2)}) %all-to-all-start.8) | async-done | bytes 4128 | tf_op jit(solution)/shard_map/all_to_all | solution.py:25
  95.8 0.6 reduce_sum.79
  (19 shorter events, 0.4 us)
Async XLA Ops:
  1.3 46.1 %copy-start = (f32[4,3,640]{2,0,1:T(4,128)S(1)}, f32[4,3,640]{2,0,1:T(4,128)}, u32[]{:S(2)}) copy-start(f32[4,3,640]{2,0,1:T(4,128)} %param.14) | copy-start | bytes 92164
  1.3 46.1 %copy-start.1 = (f32[4,3,640]{2,0,1:T(4,128)S(1)}, f32[4,3,640]{2,0,1:T(4,128)}, u32[]{:S(2)}) copy-start(f32[4,3,640]{2,0,1:T(4,128)} %param.13) | copy-start | bytes 92164
  1.4 46.1 %copy-start.2 = (f32[4,3,640]{2,0,1:T(4,128)S(1)}, f32[4,3,640]{2,0,1:T(4,128)}, u32[]{:S(2)}) copy-start(f32[4,3,640]{2,0,1:T(4,128)} %param.12) | copy-start | bytes 92164
  27.6 18.4 %all-to-all-start.3 = ((bf16[8,18,640]{2,1,0:T(8,128)(2,1)}), bf16[8,18,640]{2,1,0:T(8,128)(2,1)S(1)}, u32[]{:S(2)}, u32[]{:S(2)}) async-start(bf16[8,18,640]{2,1,0:T(8,128)(2,1)} %fold.4), calls=%async_computation.3 | async-start | bytes 491520 | tf_op jit(solution)/shard_map/cond/branch_1_fun/all_to_all | solution.py:25
  73.8 22.0 %all-to-all-start.8 = ((f32[8,1,128]{2,1,0:T(1,128)}), f32[8,1,128]{2,1,0:T(1,128)S(1)}, u32[]{:S(2)}, u32[]{:S(2)}) async-start(f32[8,1,128]{2,1,0:T(1,128)} %broadcast_in_dim.91), calls=%async_computation.8 | async-start | bytes 8192 | tf_op jit(solution)/shard_map/all_to_all | solution.py:25

commit v5 on v4

--- a/solution.py
+++ b/solution.py
@@ -88,14 +88,16 @@
 
 
 def fold_kernel(own, came, codes, rows):
-    outer, lots, block, _ = came.shape
+    outer, lots, block, cols = came.shape
     for lot in range(lots):
-        total = came[0, lot].astype(jnp.float32)
-        for k in range(1, outer):
-            total += came[k, lot].astype(jnp.float32)
-        code = encode(total)
-        for y in range(block // own):
-            rows[y, lot * own : (lot + 1) * own] = code[y * own : (y + 1) * own]
+        for col in range(0, cols, 128):
+            lanes = slice(col, col + 128)
+            terms = [came[k, lot, :, lanes].astype(jnp.float32) for k in range(outer)]
+            while len(terms) > 1:
+                terms = [a + b for a, b in zip(terms[::2], terms[1::2])]
+            code = encode(terms[0])
+            for y in range(block // own):
+                rows[y, lot * own : (lot + 1) * own, lanes] = code[y * own : (y + 1) * own]
     codes[...] = rows[...].astype(codes.dtype)
 
 
@@ -120,7 +122,7 @@
     block, own = rows // outer, rows // (outer * inner)
     shape = (layers, outer, block, cols)
     blocks, marks = pack(slots, refresh, grad_part.reshape(shape), hess_part.reshape(shape))
-    came = exchange(fold(exchange(blocks, FIRST)), "y")
+    came, marks = lax.optimization_barrier((exchange(fold(exchange(blocks, FIRST)), "y"), marks))
     sums = jnp.sum(decode(came), axis=0)
     parts = [sums[: layers * own]]
     held = [sums[(layers + s) * own : (layers + s + 1) * own] for s in range(slots)]

time: 98.6 us -> 100 us (1.014)
  blocking collectives: 48.2 us -> 68.4 us
  waiting for transfers between devices: 13.2 us -> 4.01 us
  starting transfers between devices: 24.2 us -> 15.4 us
    all_to_all x3 -> x4, blocking collectives: 48.2 us -> 68.4 us  [exchange(): lax.all_to_all(blocks, axes, split_axis=0, concat_axis=0, tiled=False)]
    all_to_all x2 -> x1, waiting for transfers between devices: 13.2 us -> 4.01 us  [exchange(): lax.all_to_all(blocks, axes, split_axis=0, concat_axis=0, tiled=False)]
    all_to_all x2 -> x1, starting transfers between devices: 24.2 us -> 15.4 us  [exchange(): lax.all_to_all(blocks, axes, split_axis=0, concat_axis=0, tiled=False)]
  transfers between devices with their start and end apart: 2 -> 1, of which waited for: 2 -> 1; matrix products, arithmetic and copies ran while one was open for 3% -> 3% of each run, Pallas kernels for 0% -> 0%
where the time goes in v5:
time: 100 us; the launch traced here: 99.9 us
  blocking collectives  68.4 us (68%)
  starting transfers between devices  15.4 us (15%)
  local copies, waits for them, and re-layouts  4.14 us (4%)
  waiting for transfers between devices  4.01 us (4%)
  between operations  3.26 us (3%)
  Pallas kernels  3.15 us (3%)
  other arithmetic  1.39 us (1%)
    all_to_all x4, blocking collectives, exchange(): lax.all_to_all(blocks, axes, split_axis=0, concat_axis=0, tiled=False)  68.4 us
    all_to_all x1, starting transfers between devices, exchange(): lax.all_to_all(blocks, axes, split_axis=0, concat_axis=0, tiled=False)  15.4 us
    all_to_all x1, waiting for transfers between devices, exchange(): lax.all_to_all(blocks, axes, split_axis=0, concat_axis=0, tiled=False)  4.01 us
    pallas_call x1, Pallas kernels, pack(): pl.pallas_call(functools.partial(pack_kernel, slots), out_shape=(pltpu.VM...  2.08 us
  transfers between devices with their start and end apart: 1, of which 1 were waited for; matrix products, arithmetic and copies ran while one was open for 3% of the time, Pallas kernels for 0%

profile of v5, /device:TPU:1, one launch (start us, length us, event | category | flops | bytes accessed | tf_op | source)
XLA Modules:
  0.0 99.9 jit_solution(7636077330259722748)
XLA Ops:
  0.6 0.7 branch.1
  1.3 0.0 copy-start
  1.3 0.0 copy-start.1
  1.4 0.0 copy-start.2
  1.4 47.4 %conditional.1 = (f32[28,640]{1,0:T(8,128)S(1)}) conditional(s32[]{:T(128)} %bitcast.6, (bf16[1,4,192,640]{3,2,1,0:T(8,128)(2,1)}, bf16[1,4,192,640]{3,2,1,0:T(8,128)(2,1)}, s32[4]{0:T(128)}) %tuple.20, (bf16[1,4,192,640]{3,2,1,0:T(8,128)(2,1)}, bf16[1,4,192,640]{3,2,1,0:T(8,128)(2,1)}, s32[4]{0:T(128)}) %tuple.20, ...), branch_computations={%region_0.2_spmd, %region_2.4_spmd, %region_4.6_spmd} | conditional | flops 752000 | bytes 4440328 | solution.py:165
  1.4 2.1 %pack.5 = (bf16[8,7,24,640]{3,2,1,0:T(8,128)(2,1)S(1)}, f32[8,640]{1,0:T(8,128)S(1)}) custom-call(s32[4]{0:T(128)} %get-tuple-element.36.refresh, bf16[4,8,24,640]{3,2,1,0:T(8,128)(2,1)} %bitcast.22, bf16[4,8,24,640]{3,2,1,0:T(8,128)(2,1)} %bitcast.25), custom_call_target="tpu_custom_call" | custom-call | tf_op jit(solution)/shard_map/cond/branch_2_fun/pack/pallas_call | solution.py:72
  3.5 25.8 %all_to_all.43.came = bf16[8,7,24,640]{3,2,1,0:T(8,128)(2,1)S(1)} all-to-all(bf16[8,7,24,640]{3,2,1,0:T(8,128)(2,1)S(1)} %get-tuple-element.39), channel_id=1, replica_groups=mesh['zl'=2,'x'=4,'y'=8,'zh'=4,'core'=2] {'zl','x'}, dimensions={0} | all-to-all | bytes 3440640 | tf_op jit(solution)/shard_map/cond/branch_2_fun/all_to_all | solution.py:25
  29.3 0.4 fold.5
  29.7 18.3 %all_to_all.44 = bf16[8,21,640]{2,1,0:T(8,128)(2,1)S(1)} all-to-all(bf16[8,21,640]{2,1,0:T(8,128)(2,1)S(1)} %fold.5), channel_id=1, replica_groups=mesh['zl'=2,'x'=4,'y'=8,'zh'=4,'core'=2] {'y'}, dimensions={0} | all-to-all | bytes 430080 | tf_op jit(solution)/shard_map/cond/branch_2_fun/all_to_all | solution.py:25
  48.0 0.1 compare_reduce_fusion.4
  48.0 0.5 fusion.14
  48.5 0.2 concatenate.15
  49.5 0.0 copy-done
  49.5 0.0 copy-done.1
  49.5 0.0 copy-done.2
  49.5 0.1 fusion.22
  49.7 10.8 %all_to_all.45 = bf16[8,16,640]{2,1,0:T(8,128)(2,1)S(1)} all-to-all(bf16[8,16,640]{2,1,0:T(8,128)(2,1)S(1)} %broadcast_in_dim.89), channel_id=1, replica_groups=mesh['zl'=2,'x'=4,'y'=8,'zh'=4,'core'=2] {'y'}, dimensions={0} | all-to-all | bytes 327680 | tf_op jit(solution)/shard_map/all_to_all | solution.py:25
  60.5 0.1 copy.60
  60.6 0.1 reshape.94
  60.8 0.1 broadcast_in_dim.90
  60.9 13.5 %all_to_all.46 = bf16[8,97,640]{2,1,0:T(8,128)(2,1)S(1)} all-to-all(bf16[8,97,640]{2,1,0:T(8,128)(2,1)S(1)} %broadcast_in_dim.90), channel_id=1, replica_groups=mesh['zl'=2,'x'=4,'y'=8,'zh'=4,'core'=2] {'zl','x'}, dimensions={0} | all-to-all | bytes 1986560 | tf_op jit(solution)/shard_map/all_to_all | solution.py:25
  74.5 0.6 broadcast_in_dim.91
  75.1 15.4 %all-to-all-start.8 = ((f32[8,1,128]{2,1,0:T(1,128)}), f32[8,1,128]{2,1,0:T(1,128)S(1)}, u32[]{:S(2)}, u32[]{:S(2)}) async-start(f32[8,1,128]{2,1,0:T(1,128)} %broadcast_in_dim.91), calls=%async_computation.8 | async-start | bytes 8192 | tf_op jit(solution)/shard_map/all_to_all | solution.py:25
  90.5 0.6 copy.63
  91.1 0.6 copy.64
  91.7 0.6 copy.65
  92.3 0.1 slice.98
  92.4 1.0 %copy.61 = bf16[4,8,24,640]{3,2,1,0:T(8,128)(2,1)} copy(bf16[4,8,24,640]{3,2,0,1:T(8,128)(2,1)S(1)} %bitcast.26) | data formatting | bytes 1966080 | tf_op jit(solution)/shard_map/transpose | solution.py:194
  93.5 4.0 %all-to-all-done.8 = f32[8,1,128]{2,1,0:T(1,128)S(1)} async-done(((f32[8,1,128]{2,1,0:T(1,128)}), f32[8,1,128]{2,1,0:T(1,128)S(1)}, u32[]{:S(2)}, u32[]{:S(2)}) %all-to-all-start.8) | async-done | bytes 4128 | tf_op jit(solution)/shard_map/all_to_all | solution.py:25
  97.5 0.6 reduce_sum.79
  (18 shorter events, 0.3 us)
Async XLA Ops:
  1.3 48.2 %copy-start = (f32[4,3,640]{2,0,1:T(4,128)S(1)}, f32[4,3,640]{2,0,1:T(4,128)}, u32[]{:S(2)}) copy-start(f32[4,3,640]{2,0,1:T(4,128)} %param.14) | copy-start | bytes 92164
  1.3 48.2 %copy-start.1 = (f32[4,3,640]{2,0,1:T(4,128)S(1)}, f32[4,3,640]{2,0,1:T(4,128)}, u32[]{:S(2)}) copy-start(f32[4,3,640]{2,0,1:T(4,128)} %param.13) | copy-start | bytes 92164
  1.4 48.2 %copy-start.2 = (f32[4,3,640]{2,0,1:T(4,128)S(1)}, f32[4,3,640]{2,0,1:T(4,128)}, u32[]{:S(2)}) copy-start(f32[4,3,640]{2,0,1:T(4,128)} %param.12) | copy-start | bytes 92164
  75.1 22.4 %all-to-all-start.8 = ((f32[8,1,128]{2,1,0:T(1,128)}), f32[8,1,128]{2,1,0:T(1,128)S(1)}, u32[]{:S(2)}, u32[]{:S(2)}) async-start(f32[8,1,128]{2,1,0:T(1,128)} %broadcast_in_dim.91), calls=%async_computation.8 | async-start | bytes 8192 | tf_op jit(solution)/shard_map/all_to_all | solution.py:25

commit v6 on v5

--- a/solution.py
+++ b/solution.py
@@ -189,13 +189,15 @@
     held = held.reshape(layers * block, cols)
     count = jnp.sum(came[:, layers * own].astype(jnp.float32), axis=0)[None]
 
-    load = jnp.concatenate([held, count.astype(jnp.bfloat16)], axis=0)
+    held = held.reshape(-1, 8, cols // 128, 128).transpose(0, 2, 1, 3).reshape(-1, 128)
+    load = jnp.concatenate([held, count.astype(jnp.bfloat16).reshape(-1, 128)], axis=0)
     came = exchange(jnp.broadcast_to(load[None], (outer,) + load.shape), FIRST)
-    weights = came[:, : layers * block].reshape(outer, layers, block, cols).transpose(1, 0, 2, 3)
-    weights = weights.reshape(layers, rows, cols)
-    count = jnp.sum(came[:, layers * block].astype(jnp.float32), axis=0)
-
-    count = jnp.sum(count.reshape(cols // 128, 128), axis=0)
+    size = held.shape[0]
+    weights = came[:, :size].reshape(outer, layers, block // 8, cols // 128, 8, 128)
+    weights = weights.transpose(1, 0, 2, 4, 3, 5).reshape(layers, rows, cols)
+    count = jnp.sum(came[:, size:].astype(jnp.float32), axis=0)
+
+    count = jnp.sum(count, axis=0)
     came = exchange(jnp.broadcast_to(count[None, None], (ZH * CORE, 1, 128)), TENSOR)
     total = jnp.sum(came)
     entries = layers * rows * cols * ZH * CORE

time: 100 us -> 98 us (0.980); the launches traced: 99.9 us -> 98.9 us
  no operation moved by 1% of the time
where the time goes in v6:
time: 98 us; the launch traced here: 98.9 us
  blocking collectives  67.6 us (69%)
  starting transfers between devices  15.3 us (16%)
  local copies, waits for them, and re-layouts  4.19 us (4%)
  waiting for transfers between devices  4.03 us (4%)
  between operations  3.26 us (3%)
  Pallas kernels  3.15 us (3%)
  other arithmetic  1.36 us (1%)
    all_to_all x4, blocking collectives, exchange(): lax.all_to_all(blocks, axes, split_axis=0, concat_axis=0, tiled=False)  67.6 us
    all_to_all x1, starting transfers between devices, exchange(): lax.all_to_all(blocks, axes, split_axis=0, concat_axis=0, tiled=False)  15.3 us
    all_to_all x1, waiting for transfers between devices, exchange(): lax.all_to_all(blocks, axes, split_axis=0, concat_axis=0, tiled=False)  4.03 us
    pallas_call x1, Pallas kernels, pack(): pl.pallas_call(functools.partial(pack_kernel, slots), out_shape=(pltpu.VM...  2.08 us
  transfers between devices with their start and end apart: 1, of which 1 were waited for; matrix products, arithmetic and copies ran while one was open for 3% of the time, Pallas kernels for 0%

profile of v6, /device:TPU:1, one launch (start us, length us, event | category | flops | bytes accessed | tf_op | source)
XLA Modules:
  0.0 98.9 jit_solution(5613095713102917955)
XLA Ops:
  0.6 0.7 branch.1
  1.3 0.0 copy-start
  1.3 0.0 copy-start.1
  1.4 0.0 copy-start.2
  1.4 47.4 %conditional.1 = (f32[28,640]{1,0:T(8,128)S(1)}) conditional(s32[]{:T(128)} %bitcast.6, (bf16[1,4,192,640]{3,2,1,0:T(8,128)(2,1)}, bf16[1,4,192,640]{3,2,1,0:T(8,128)(2,1)}, s32[4]{0:T(128)}) %tuple.20, (bf16[1,4,192,640]{3,2,1,0:T(8,128)(2,1)}, bf16[1,4,192,640]{3,2,1,0:T(8,128)(2,1)}, s32[4]{0:T(128)}) %tuple.20, ...), branch_computations={%region_0.2_spmd, %region_2.4_spmd, %region_4.6_spmd} | conditional | flops 752000 | bytes 4440328 | solution.py:165
  1.4 2.1 %pack.5 = (bf16[8,7,24,640]{3,2,1,0:T(8,128)(2,1)S(1)}, f32[8,640]{1,0:T(8,128)S(1)}) custom-call(s32[4]{0:T(128)} %get-tuple-element.36.refresh, bf16[4,8,24,640]{3,2,1,0:T(8,128)(2,1)} %bitcast.23, bf16[4,8,24,640]{3,2,1,0:T(8,128)(2,1)} %bitcast.26), custom_call_target="tpu_custom_call" | custom-call | tf_op jit(solution)/shard_map/cond/branch_2_fun/pack/pallas_call | solution.py:72
  3.5 25.8 %all_to_all.43.came = bf16[8,7,24,640]{3,2,1,0:T(8,128)(2,1)S(1)} all-to-all(bf16[8,7,24,640]{3,2,1,0:T(8,128)(2,1)S(1)} %get-tuple-element.39), channel_id=1, replica_groups=mesh['zl'=2,'x'=4,'y'=8,'zh'=4,'core'=2] {'zl','x'}, dimensions={0} | all-to-all | bytes 3440640 | tf_op jit(solution)/shard_map/cond/branch_2_fun/all_to_all | solution.py:25
  29.3 0.4 fold.5
  29.7 18.3 %all_to_all.44 = bf16[8,21,640]{2,1,0:T(8,128)(2,1)S(1)} all-to-all(bf16[8,21,640]{2,1,0:T(8,128)(2,1)S(1)} %fold.5), channel_id=1, replica_groups=mesh['zl'=2,'x'=4,'y'=8,'zh'=4,'core'=2] {'y'}, dimensions={0} | all-to-all | bytes 430080 | tf_op jit(solution)/shard_map/cond/branch_2_fun/all_to_all | solution.py:25
  48.0 0.1 compare_reduce_fusion.4
  48.0 0.5 fusion.14
  48.5 0.2 concatenate.15
  49.5 0.0 copy-done
  49.5 0.0 copy-done.1
  49.5 0.0 copy-done.2
  49.5 0.1 fusion.21
  49.7 10.8 %all_to_all.45 = bf16[8,16,640]{2,1,0:T(8,128)(2,1)S(1)} all-to-all(bf16[8,16,640]{2,1,0:T(8,128)(2,1)S(1)} %broadcast_in_dim.89), channel_id=1, replica_groups=mesh['zl'=2,'x'=4,'y'=8,'zh'=4,'core'=2] {'y'}, dimensions={0} | all-to-all | bytes 327680 | tf_op jit(solution)/shard_map/all_to_all | solution.py:25
  60.5 0.1 copy.64
  60.6 0.1 reshape_reshape.3
  60.8 0.1 broadcast_in_dim.90
  60.9 12.7 %all_to_all.46 = bf16[8,485,128]{2,1,0:T(8,128)(2,1)S(1)} all-to-all(bf16[8,485,128]{2,1,0:T(8,128)(2,1)S(1)} %broadcast_in_dim.90), channel_id=1, replica_groups=mesh['zl'=2,'x'=4,'y'=8,'zh'=4,'core'=2] {'zl','x'}, dimensions={0} | all-to-all | bytes 1986560 | tf_op jit(solution)/shard_map/all_to_all | solution.py:25
  73.7 0.6 broadcast_in_dim.91
  74.3 15.3 %all-to-all-start.8 = ((f32[8,1,128]{2,1,0:T(1,128)}), f32[8,1,128]{2,1,0:T(1,128)S(1)}, u32[]{:S(2)}, u32[]{:S(2)}) async-start(f32[8,1,128]{2,1,0:T(1,128)} %broadcast_in_dim.91), calls=%async_computation.8 | async-start | bytes 8192 | tf_op jit(solution)/shard_map/all_to_all | solution.py:25
  89.6 0.6 copy.68
  90.2 0.6 copy.69
  90.8 0.6 copy.70
  91.4 0.1 slice.98
  91.5 1.0 %copy.66 = bf16[4,8,3,8,5,128]{5,3,4,2,1,0:T(8,128)(2,1)} copy(bf16[4,8,3,8,5,128]{5,3,4,2,0,1:T(8,128)(2,1)S(1)} %bitcast.27) | data formatting | bytes 1966080 | tf_op jit(solution)/shard_map/transpose | solution.py:197
  92.5 4.0 %all-to-all-done.8 = f32[8,1,128]{2,1,0:T(1,128)S(1)} async-done(((f32[8,1,128]{2,1,0:T(1,128)}), f32[8,1,128]{2,1,0:T(1,128)S(1)}, u32[]{:S(2)}, u32[]{:S(2)}) %all-to-all-start.8) | async-done | bytes 4128 | tf_op jit(solution)/shard_map/all_to_all | solution.py:25
  96.6 0.6 reduce_sum.73
  (17 shorter events, 0.3 us)
Async XLA Ops:
  1.3 48.2 %copy-start = (f32[4,3,640]{2,0,1:T(4,128)S(1)}, f32[4,3,640]{2,0,1:T(4,128)}, u32[]{:S(2)}) copy-start(f32[4,3,640]{2,0,1:T(4,128)} %param.14) | copy-start | bytes 92164
  1.3 48.2 %copy-start.1 = (f32[4,3,640]{2,0,1:T(4,128)S(1)}, f32[4,3,640]{2,0,1:T(4,128)}, u32[]{:S(2)}) copy-start(f32[4,3,640]{2,0,1:T(4,128)} %param.13) | copy-start | bytes 92164
  1.4 48.2 %copy-start.2 = (f32[4,3,640]{2,0,1:T(4,128)S(1)}, f32[4,3,640]{2,0,1:T(4,128)}, u32[]{:S(2)}) copy-start(f32[4,3,640]{2,0,1:T(4,128)} %param.12) | copy-start | bytes 92164
  74.3 22.3 %all-to-all-start.8 = ((f32[8,1,128]{2,1,0:T(1,128)}), f32[8,1,128]{2,1,0:T(1,128)S(1)}, u32[]{:S(2)}, u32[]{:S(2)}) async-start(f32[8,1,128]{2,1,0:T(1,128)} %broadcast_in_dim.91), calls=%async_computation.8 | async-start | bytes 8192 | tf_op jit(solution)/shard_map/all_to_all | solution.py:25
